TPU v7x, 256 devices: a whole 4x4x8 slice. The times are simulated.
256 devices in a mesh: dp: 16 (over z, core), tensor: 16 (over y, x).
Axes of the slice: x: 4, y: 4, z: 8, core: 2. Of those that a mesh axis runs over, the one named last changes fastest.
Arguments:
- questions: bfloat16 [16, 32, 4096], P('dp', None, 'tensor'), may hold values from -30 to 30
- memory: bfloat16 [256, 128, 4096], P('dp', None, 'tensor'), may hold values from -30 to 30
- retrieved: int32 [16, 14], P('dp'), may hold values from 0 to 255, as said below
- location: int32 [256], replicated, may hold values from 0 to 255, as said below
- norm_gain: float32 [4096], replicated, may hold values from 0.1 to 1.9
- w_query: bfloat16 [4096, 4096], P(None, 'tensor'), may hold values from -0.75 to 0.75
- w_key: bfloat16 [4096, 4096], P(None, 'tensor'), may hold values from -0.75 to 0.75
- w_value: bfloat16 [4096, 4096], P(None, 'tensor'), may hold values from -0.09375 to 0.09375
- w_out: bfloat16 [4096, 4096], P('tensor'), may hold values from -0.125 to 0.125
Outputs:
- updated: bfloat16 [16, 14, 32, 4096], P('dp', None, None, 'tensor')
Inputs may be any that keep to these rules, and one draw needn't show every extreme that they name: A permutation: passage p is held in row location[p] of memory, on dp index location[p] // 16. `retrieved`: the 14 passages named by the questions of one dp index are distinct; at most 2 of them are held by one dp index, and exactly 2 by some dp index.
All inputs are finite; a program needn't handle non-finite values.
Results may differ from a plain program's by a relative error of at most 0.009.
Values may be sent and summed in bfloat16 or wider, within the bound.
A program may use at most 128 MiB of HBM per device.

v0:
```python
import jax
import jax.numpy as jnp
from jax import lax
from jax.sharding import PartitionSpec as P

HEAD_DIM = 64


epsilon = 1e-06


def on_device(questions, memory, retrieved, location, norm_gain, w_query, w_key, w_value, w_out):
    question_count, question_tokens, slice_width = questions.shape
    held_count, passage_tokens, _ = memory.shape
    retrieved_count = retrieved.shape[1]
    requests = question_count * retrieved_count
    wanted = retrieved.reshape(requests)
    every_request = lax.all_gather(wanted, "dp", axis=0, tiled=True)
    stored = location[every_request]
    held_here = stored // held_count == lax.axis_index("dp")
    local_rows = stored % held_count
    picked = memory[local_rows]
    masked = jnp.where(held_here[:, None, None], picked, jnp.zeros((), jnp.bfloat16))
    fetched = lax.psum_scatter(
        masked.astype(jnp.float32).astype(jnp.bfloat16), "dp", scatter_dimension=0, tiled=True
    )
    question_rows = questions.reshape(question_count * question_tokens, slice_width)
    passage_rows = fetched.reshape(requests * passage_tokens, slice_width)
    heads_width = w_key.shape[1]
    heads_local = heads_width // HEAD_DIM
    widened_question = question_rows.astype(jnp.float32)
    widened_passage = passage_rows.astype(jnp.float32)
    squares_question, squares_passage = lax.psum(
        (
            jnp.sum(widened_question * widened_question, axis=1),
            jnp.sum(widened_passage * widened_passage, axis=1),
        ),
        "tensor",
    )
    normed_question = (
        lax.all_gather(question_rows, "tensor", axis=1, tiled=True).astype(jnp.float32) * norm_gain
    ).astype(jnp.bfloat16)
    normed_passage = (
        lax.all_gather(passage_rows, "tensor", axis=1, tiled=True).astype(jnp.float32) * norm_gain
    ).astype(jnp.bfloat16)
    full_width = norm_gain.shape[0]
    scale_question = lax.rsqrt(squares_question / full_width + epsilon)[:, None]
    scale_passage = lax.rsqrt(squares_passage / full_width + epsilon)[:, None]
    query_rows = (
        (jnp.dot(normed_question, w_query, preferred_element_type=jnp.float32) * scale_question)
        .astype(jnp.bfloat16)
        .reshape(question_count, question_tokens, heads_local, HEAD_DIM)
    )
    key_question = (
        (jnp.dot(normed_question, w_key, preferred_element_type=jnp.float32) * scale_question)
        .astype(jnp.bfloat16)
        .reshape(question_count, question_tokens, heads_local, HEAD_DIM)
    )
    value_question = (
        (jnp.dot(normed_question, w_value, preferred_element_type=jnp.float32) * scale_question)
        .astype(jnp.bfloat16)
        .reshape(question_count, question_tokens, heads_local, HEAD_DIM)
    )
    key_passage = (
        (jnp.dot(normed_passage, w_key, preferred_element_type=jnp.float32) * scale_passage)
        .astype(jnp.bfloat16)
        .reshape(question_count, retrieved_count, passage_tokens, heads_local, HEAD_DIM)
    )
    value_passage = (
        (jnp.dot(normed_passage, w_value, preferred_element_type=jnp.float32) * scale_passage)
        .astype(jnp.bfloat16)
        .reshape(question_count, retrieved_count, passage_tokens, heads_local, HEAD_DIM)
    )
    score_scale = HEAD_DIM ** (-0.5)
    own_scores = (
        jnp.einsum("athd,ashd->ahts", query_rows, key_question, preferred_element_type=jnp.float32)
        * score_scale
    )
    far_scores = (
        jnp.einsum("athd,akshd->akhts", query_rows, key_passage, preferred_element_type=jnp.float32)
        * score_scale
    )
    own_scores = jnp.broadcast_to(
        own_scores[:, None],
        (question_count, retrieved_count, heads_local, question_tokens, question_tokens),
    )
    scores = jnp.concatenate([own_scores, far_scores], axis=-1)
    attention = jax.nn.softmax(scores, axis=-1).astype(jnp.bfloat16)
    context = jnp.einsum(
        "akhts,ashd->akthd",
        attention[..., :question_tokens],
        value_question,
        preferred_element_type=jnp.float32,
    )
    context = context + jnp.einsum(
        "akhts,akshd->akthd",
        attention[..., question_tokens:],
        value_passage,
        preferred_element_type=jnp.float32,
    )
    context = context.astype(jnp.bfloat16).reshape(requests * question_tokens, heads_width)
    head_term = jnp.dot(context, w_out, preferred_element_type=jnp.float32)
    summed = lax.psum(head_term.astype(jnp.bfloat16), "tensor").astype(jnp.float32)
    own_share = lax.dynamic_slice_in_dim(
        summed, lax.axis_index("tensor") * slice_width, slice_width, 1
    )
    own_share = own_share.reshape(question_count, retrieved_count, question_tokens, slice_width)
    result = questions.astype(jnp.float32)[:, None] + own_share
    return result.astype(jnp.bfloat16)


def solution(mesh):
    placed = (
        P("dp", None, "tensor"),
        P("dp", None, "tensor"),
        P("dp", None),
        P(),
        P(),
        P(None, "tensor"),
        P(None, "tensor"),
        P(None, "tensor"),
        P("tensor", None),
    )
    return jax.shard_map(
        on_device,
        mesh=mesh,
        in_specs=placed,
        out_specs=P("dp", None, None, "tensor"),
        check_vma=False,
    )
```

profile of v0, /device:TPU:32, one launch (start us, length us, event | category | flops | bytes accessed | tf_op | source)
XLA Modules:
  0.0 405.4 jit_solution(13121945573946188596)
XLA Ops:
  6.5 1.4 dynamic-slice
  8.6 0.8 bitcast_dynamic-update-slice_fusion
  9.4 15.4 %all-reduce = s32[224]{0:T(256)S(1)} all-reduce(s32[224]{0:T(256)S(1)} %bitcast_dynamic-update-slice_fusion), channel_id=3, replica_groups=mesh['dp'=16,'tensor'=16] {'dp'}, use_global_device_ids=true, to_apply=%add | all-reduce | flops 224 | bytes 1792 | tf_op jit(solution)/shard_map/all_gather | solution.py:18
  24.8 2.0 gather_fusion
  26.8 9.2 %gather_fusion.1 = bf16[224,128,256]{2,1,0:T(8,128)(2,1)} fusion(bf16[16,128,256]{2,1,0:T(8,128)(2,1)S(1)} %copy-done.1, s32[1024]{0:T(1024)S(1)} %pad_clamp_fusion), kind=kCustom, calls=%fused_computation.1 | custom fusion | bytes 29361024 | tf_op jit(solution)/shard_map/gather | solution.py:22
  36.0 13.5 %broadcast_select_fusion = bf16[224,128,256]{2,1,0:T(8,128)(2,1)} fusion(bf16[224,128,256]{2,1,0:T(8,128)(2,1)} %gather_fusion.1, pred[224]{0:T(512)(128)(4,1)S(1)} %fusion.35), kind=kLoop, calls=%fused_computation.3 | loop fusion | flops 7340032 | bytes 29360352 | tf_op jit(solution)/shard_map/jit(_where)/select_n | solution.py:23
  49.6 85.1 %reduce-scatter.2.cloned.1.call-done = bf16[14,128,256]{2,1,0:T(8,128)(2,1)} async-done(((bf16[224,128,256]{2,1,0:T(8,128)(2,1)}), bf16[14,128,256]{2,1,0:T(8,128)(2,1)}) %reduce-scatter.2.cloned.1.call-update) | async-done | bytes 917520 | tf_op jit(solution)/shard_map/reduce_scatter | solution.py:24
  134.8 25.2 %all-gather = bf16[1,32,4096]{2,1,0:T(8,128)(2,1)S(1)} all-gather(bf16[1,32,256]{2,1,0:T(8,128)(2,1)S(1)} %copy-done.4), channel_id=2, replica_groups=mesh['dp'=16,'tensor'=16] {'tensor'}, dimensions={2}, use_global_device_ids=true | all-gather | bytes 278528 | tf_op jit(solution)/shard_map/all_gather | solution.py:41
  160.0 0.1 multiply_reduce_fusion.1
  160.1 1.5 multiply_reduce_fusion
  161.6 39.9 %all-reduce.1 = (f32[1792]{0:T(1024)S(1)}, f32[32]{0:T(128)S(1)}) all-reduce(f32[1792]{0:T(1024)S(1)} %bitcast.54, f32[32]{0:T(128)S(1)} %multiply_reduce_fusion.1), channel_id=1, replica_groups=mesh['dp'=16,'tensor'=16] {'tensor'}, use_global_device_ids=true, to_apply=%region_4.5 | all-reduce | flops 1824 | bytes 14592 | tf_op jit(solution)/shard_map/psum | solution.py:33
  201.6 2.0 fusion.24
  203.7 2.0 fusion.25
  205.8 2.0 fusion.23
  207.9 0.1 convolution_multiply_fusion
  208.0 0.3 broadcast_reduce_fusion
  208.3 46.9 %all-gather.4.cloned.1.call-done = bf16[1792,4096]{1,0:T(8,128)(2,1)} async-done(((bf16[1792,256]{1,0:T(8,128)(2,1)}), bf16[1792,4096]{1,0:T(8,128)(2,1)}) %all-gather.4.cloned.1.call-update) | async-done | bytes 14680080 | tf_op jit(solution)/shard_map/all_gather | solution.py:44
  255.3 9.9 %fusion.4 = bf16[1792,256]{1,0:T(8,128)(2,1)S(1)} fusion(bf16[4096,256]{1,0:T(8,128)(2,1)} %param.16, bf16[1792,4096]{1,0:T(8,128)(2,1)} %all-gather.4.cloned.1.call-done, f32[4096]{0:T(1024)S(1)} %copy-done.3, f32[1792]{0:T(1024)S(1)} %add_rsqrt_fusion), kind=kOutput, calls=%fused_computation.9 | convolution fusion | flops 3781033984 | bytes 17718272 | tf_op jit(solution)/shard_map/dot_general | solution.py:70
  265.2 1.9 reshape.253
  267.1 9.9 %fusion.5 = bf16[1792,256]{1,0:T(8,128)(2,1)S(1)} fusion(bf16[4096,256]{1,0:T(8,128)(2,1)} %param.15, bf16[1792,4096]{1,0:T(8,128)(2,1)} %all-gather.4.cloned.1.call-done, f32[4096]{0:T(1024)S(1)} %copy-done.3, f32[1792]{0:T(1024)S(1)} %add_rsqrt_fusion), kind=kOutput, calls=%fused_computation.10 | convolution fusion | flops 3781033984 | bytes 17718272 | tf_op jit(solution)/shard_map/dot_general | solution.py:65
  277.1 1.7 reshape.252
  278.8 2.3 fusion.36
  281.2 1.1 fusion.11
  282.4 1.2 divide_convert_fusion
  283.6 0.6 fusion.12
  284.2 0.3 fusion.22
  284.5 0.4 copy.28
  284.9 0.3 reshape.221
  285.2 3.0 convolution_convert_fusion
  288.2 109.0 %all-reduce.4.cloned.1.call-done = bf16[448,4096]{1,0:T(8,128)(2,1)} async-done(((bf16[448,4096]{1,0:T(8,128)(2,1)}), bf16[448,4096]{1,0:T(8,128)(2,1)}) %all-reduce.4.cloned.1.call-update) | async-done | bytes 3670032 | tf_op jit(solution)/shard_map/psum | solution.py:103
  397.2 1.0 dynamic-slice_convert_fusion
  398.1 0.7 add_convert_fusion
  (30 shorter events, 0.6 us)
Async XLA Ops:
  6.5 278.7 %copy-start = (bf16[256,4096]{1,0:T(8,128)(2,1)S(1)}, bf16[256,4096]{1,0:T(8,128)(2,1)}, u32[]{:S(2)}) copy-start(bf16[256,4096]{1,0:T(8,128)(2,1)} %param.17) | copy-start | bytes 6291460
  6.5 20.3 %copy-start.1 = (bf16[16,128,256]{2,1,0:T(8,128)(2,1)S(1)}, bf16[16,128,256]{2,1,0:T(8,128)(2,1)}, u32[]{:S(2)}) copy-start(bf16[16,128,256]{2,1,0:T(8,128)(2,1)} %param.10) | copy-start | bytes 3145732
  6.5 128.2 %reduce-scatter.2.cloned.1.call-start = ((), (), s32[]{:S(2)}) async-start(), calls=%async_computation.1 | async-start | bytes 15597568 | tf_op jit(solution)/shard_map/reduce_scatter | solution.py:24
  49.5 85.3 %copy-start.4 = (bf16[1,32,256]{2,1,0:T(8,128)(2,1)S(1)}, bf16[1,32,256]{2,1,0:T(8,128)(2,1)}, u32[]{:S(2)}) copy-start(bf16[1,32,256]{2,1,0:T(8,128)(2,1)} %param.9) | copy-start | bytes 49156
  49.5 152.0 %copy-start.3 = (f32[4096]{0:T(1024)S(1)}, f32[4096]{0:T(1024)}, u32[]{:S(2)}) copy-start(f32[4096]{0:T(1024)} %param.13) | copy-start | bytes 49156
  49.5 205.8 %all-gather.4.cloned.1.call-start = ((), (), s32[]{:S(2)}) async-start(), calls=%async_computation.2 | async-start | bytes 15597568 | tf_op jit(solution)/shard_map/all_gather | solution.py:44
  134.7 262.4 %all-reduce.4.cloned.1.call-start = ((), (), s32[]{:S(2)}) async-start(), calls=%async_computation.3 | async-start | bytes 7340032 | tf_op jit(solution)/shard_map/psum | solution.py:103
  281.2 2.4 copy-start.2
Sparse Core Ops, SparseCore 0:
  49.6 85.0 reduce-scatter.1
  137.1 118.1 all-gather.3
  288.3 108.8 all-reduce.3
where the time goes:
time: 407 us; the launch traced here: 405 us
  waiting for transfers between devices  241 us (59%)
  blocking collectives  80.5 us (20%)
  matrix products  32.2 us (8%)
  other arithmetic  19.5 us (5%)
  local copies, waits for them, and re-layouts  18 us (4%)
  between operations  14 us (3%)
    psum x1, waiting for transfers between devices, on_device(): lax.psum(head_term.astype(jnp.bfloat16), 'tensor').astype(jnp.float32)  109 us
    reduce_scatter x1, waiting for transfers between devices, on_device(): lax.psum_scatter(masked.astype(jnp.float32).astype(jnp.bfloat16), 'dp', s...  85.1 us
    all_gather x1, waiting for transfers between devices, on_device(): lax.all_gather(passage_rows, 'tensor', axis=1, tiled=True)  46.9 us
    psum x1, blocking collectives, on_device(): lax.psum((jnp.sum(widened_question * widened_question, axis=1), jnp.sum(w...  39.9 us
    all_gather x1, blocking collectives, on_device(): lax.all_gather(question_rows, 'tensor', axis=1, tiled=True)  25.2 us
    all_gather x1, blocking collectives, on_device(): every_request = lax.all_gather(wanted, 'dp', axis=0, tiled=True)  15.4 us
    select_n x1, other arithmetic, on_device(): jnp.where(held_here[:, None, None], picked, jnp.zeros((), jnp.bfloat16))  13.5 us
    dot_general x1, matrix products, on_device(): jnp.dot(normed_passage, w_value, preferred_element_type=jnp.float32)  9.94 us
  transfers between devices with their start and end apart: 3, of which 3 were waited for; matrix products, arithmetic and copies ran while one was open for 2% of the time, Pallas kernels for 0%

commit v1 on v0

v1 whole, which is shorter than its diff:
```python
import functools

import jax
import jax.numpy as jnp
from jax import lax
from jax.experimental import pallas as pl
from jax.experimental.pallas import tpu as pltpu
from jax.sharding import PartitionSpec as P

HEAD_DIM = 64
SIDE = 4
PIECES = 4
SLOTS = 2
epsilon = 1e-06
MESH = pl.DeviceIdType.MESH
f32 = jnp.float32
bf16 = jnp.bfloat16


def attend_kernel(
    n_dp,
    n_tp,
    retrieved_ref,
    location_ref,
    questions_ref,
    memory_ref,
    gain_ref,
    wq_hbm,
    wk_hbm,
    wv_hbm,
    context_ref,
    table,
    tables,
    tables_s,
    place_s,
    outbox,
    inbox0,
    inbox1,
    inbox2,
    inbox3,
    gathered,
    asked,
    wq,
    wkv,
    total,
    squares,
    asked_total,
    asked_squares,
    keys,
    values,
    w_sem,
    tables_sem,
    table_send,
    table_recv,
    asked_send,
    asked_recv,
    fetch_send,
    fetch_recv,
    ring_send,
    ring_recv,
):
    inboxes = (inbox0, inbox1, inbox2, inbox3)
    held, tokens, width = memory_ref.shape
    question_tokens = questions_ref.shape[0]
    requests = retrieved_ref.shape[1]
    piece = tokens // PIECES
    rows = requests * piece
    half = rows // 2
    quarter = rows // 4
    full_width = n_tp * width
    heads = width // HEAD_DIM
    d = lax.axis_index("dp")
    t = lax.axis_index("tensor")
    x, y = lax.rem(t, SIDE), lax.div(t, SIDE)

    def at(dx, dy):
        return lax.rem(y + dy + SIDE, SIDE) * SIDE + lax.rem(x + dx + SIDE, SIDE)

    w_copies = [
        pltpu.make_async_copy(wq_hbm, wq, w_sem.at[0]),
        pltpu.make_async_copy(wk_hbm, wkv.at[:, :, pl.ds(0, width)], w_sem.at[1]),
        pltpu.make_async_copy(wv_hbm, wkv.at[:, :, pl.ds(width, width)], w_sem.at[2]),
    ]
    for copy in w_copies:
        copy.start()

    barrier = pltpu.get_barrier_semaphore()

    @pl.loop(1, n_dp)
    def _(k):
        pl.semaphore_signal(barrier, inc=1, device_id={"dp": lax.rem(d + k, n_dp)}, device_id_type=MESH)

    @pl.loop(1, n_tp)
    def _(k):
        pl.semaphore_signal(barrier, inc=1, device_id={"tensor": lax.rem(t + k, n_tp)}, device_id_type=MESH)

    stored = [location_ref[retrieved_ref[0, j]] for j in range(requests)]
    owners = [s // held for s in stored]
    local = [s % held for s in stored]
    lane = lax.broadcasted_iota(jnp.int32, (8, 128), 1)
    first = jnp.zeros((8, 128), jnp.int32)
    last = jnp.zeros((8, 128), jnp.int32)
    for j in range(requests):
        last = jnp.where(lane == owners[j], local[j], last)
    for j in reversed(range(requests)):
        first = jnp.where(lane == owners[j], local[j], first)
    sub = lax.broadcasted_iota(jnp.int32, (8, 128), 0)
    table[...] = jnp.where(sub == 0, first, last)
    for j in range(requests):
        again = jnp.int32(0)
        for i in range(j):
            again = jnp.where(owners[i] == owners[j], jnp.int32(1), again)
        place_s[j] = owners[j] * SLOTS + again

    tables[pl.ds(d, 1)] = table[...][None]
    asked[pl.ds(t, 1)] = questions_ref[...][None]

    pl.semaphore_wait(barrier, n_dp + n_tp - 2)

    def table_copy(k):
        return pltpu.make_async_remote_copy(
            src_ref=table,
            dst_ref=tables.at[d],
            send_sem=table_send.at[k],
            recv_sem=table_recv.at[k],
            device_id={"dp": lax.rem(d + k, n_dp)},
            device_id_type=MESH,
        )

    def asked_copy(k):
        return pltpu.make_async_remote_copy(
            src_ref=questions_ref,
            dst_ref=asked.at[t],
            send_sem=asked_send.at[k],
            recv_sem=asked_recv.at[k],
            device_id={"tensor": lax.rem(t + k, n_tp)},
            device_id_type=MESH,
        )

    def table_arrival(k):
        return pltpu.make_async_remote_copy(
            src_ref=table,
            dst_ref=tables.at[lax.rem(d + n_dp - k, n_dp)],
            send_sem=table_send.at[k],
            recv_sem=table_recv.at[k],
            device_id={"dp": lax.rem(d + k, n_dp)},
            device_id_type=MESH,
        )

    def asked_arrival(k):
        return pltpu.make_async_remote_copy(
            src_ref=questions_ref,
            dst_ref=asked.at[lax.rem(t + n_tp - k, n_tp)],
            send_sem=asked_send.at[k],
            recv_sem=asked_recv.at[k],
            device_id={"tensor": lax.rem(t + k, n_tp)},
            device_id_type=MESH,
        )

    @pl.loop(1, n_dp)
    def _(k):
        table_copy(k).start()

    @pl.loop(1, n_tp)
    def _(k):
        asked_copy(k).start()

    @pl.loop(1, n_dp)
    def _(k):
        table_arrival(k).wait_recv()

    to_scalar = pltpu.make_async_copy(tables, tables_s, tables_sem)
    to_scalar.start()
    to_scalar.wait()

    def fetch_copy(c, k, sender):
        return pltpu.make_async_remote_copy(
            src_ref=outbox.at[c, k],
            dst_ref=inboxes[c].at[pl.ds(sender * SLOTS, SLOTS)],
            send_sem=fetch_send.at[c, k],
            recv_sem=fetch_recv.at[c, k],
            device_id={"dp": lax.rem(d + k, n_dp)},
            device_id_type=MESH,
        )

    for c in range(PIECES):
        span = pl.ds(c * piece, piece)

        @pl.loop(1, n_dp)
        def _(k):
            asker = lax.rem(d + k, n_dp)
            for s in range(SLOTS):
                outbox[c, k, s] = memory_ref[tables_s[asker, s, d], span, :]
            fetch_copy(c, k, d).start()

        for s in range(SLOTS):
            inboxes[c][pl.ds(d * SLOTS + s, 1)] = memory_ref[tables_s[d, s, d], span, :][None]

    for copy in w_copies:
        copy.wait()

    @pl.loop(1, n_tp)
    def _(k):
        asked_arrival(k).wait_recv()

    asked_total[...] = jnp.zeros_like(asked_total)
    asked_squares[...] = jnp.zeros_like(asked_squares)

    @pl.loop(0, n_tp)
    def _(s):
        wide = asked[s].astype(f32)
        normed = (wide * gain_ref[pl.ds(s, 1), :]).astype(bf16)
        asked_squares[...] += jnp.sum(wide * wide, axis=1, keepdims=True)
        asked_total[:, :width] += jnp.dot(normed, wq[s], preferred_element_type=f32)
        asked_total[:, width:] += jnp.dot(normed, wkv[s], preferred_element_type=f32)

    asked_scale = lax.rsqrt(asked_squares[:, :1] / full_width + epsilon)
    projected = (asked_total[...] * asked_scale).astype(bf16)
    own_query = projected[:, :width] * jnp.asarray(HEAD_DIM ** (-0.5), bf16)
    own_key = projected[:, width : 2 * width]
    own_value = projected[:, 2 * width :]
    head_of = lax.broadcasted_iota(jnp.int32, (question_tokens, width), 1) // HEAD_DIM
    spread = jnp.concatenate(
        [jnp.where(head_of == h, own_query, jnp.zeros_like(own_query)) for h in range(heads)], axis=0
    )

    def dot_t(a, b):
        return lax.dot_general(a, b, (((1,), (1,)), ((), ())), preferred_element_type=f32)

    own_scores = dot_t(spread, own_key)
    own_most = jnp.max(own_scores, axis=1, keepdims=True)

    def ring(c, kind, h, direction, k, arrival):
        sign = 1 if direction == 0 else -1
        mine = 0 if not arrival else -sign
        if kind in ("own", "pass"):
            step = (sign, 0) if h == 0 else (0, sign)
            back = (mine, 0) if h == 0 else (0, mine)
            if kind == "own":
                origin = at(*back)
            else:
                origin = at(*(tuple(b - s for b, s in zip(back, step))))
            index = {"own": 0, "pass": 2}[kind] + direction
        else:
            step = (0, sign) if h == 0 else (sign, 0)
            back = (0, mine) if h == 0 else (mine, 0)
            if kind == "turnpass":
                back = tuple(b - s for b, s in zip(back, step))
            shift = (k, 0) if h == 0 else (0, k)
            origin = at(*(b + s for b, s in zip(back, shift)))
            index = {"turn": 4, "turnpass": 12}[kind] + direction * 4 + k % 4
        if kind in ("pass", "turnpass"):
            span = pl.ds(h * half + direction * quarter, quarter)
        else:
            span = pl.ds(h * half, half)
        place = gathered.at[c, origin, span]
        return pltpu.make_async_remote_copy(
            src_ref=place,
            dst_ref=place,
            send_sem=ring_send.at[c, h * 20 + index],
            recv_sem=ring_recv.at[c, h * 20 + index],
            device_id={"tensor": at(*step)},
            device_id_type=MESH,
        )

    def begin(c):
        @pl.loop(1, n_dp)
        def _(k):
            fetch_copy(c, k, lax.rem(d + n_dp - k, n_dp)).wait_recv()

        for j in range(requests):
            gathered[c, pl.ds(t, 1), j * piece : (j + 1) * piece] = inboxes[c][place_s[j]][None]
        for h in range(2):
            for direction in range(2):
                ring(c, "own", h, direction, 0, False).start()
        for h in range(2):
            for direction in range(2):
                ring(c, "turn", h, direction, 0, False).start()

    def middle(c):
        for direction in range(2):
            k = -1 if direction == 0 else 1
            for h in range(2):
                ring(c, "own", h, direction, 0, True).wait_recv()
                ring(c, "pass", h, direction, 0, False).start()
                for turned in range(2):
                    ring(c, "turn", h, turned, k, False).start()
        for h in range(2):
            for direction in range(2):
                ring(c, "pass", h, direction, 0, True).wait_recv()
            for turned in range(2):
                ring(c, "turn", h, turned, 2, False).start()

    def turn_arrivals(c, k):
        for direction in range(2):
            for h in range(2):
                ring(c, "turn", h, direction, k, True).wait_recv()
                ring(c, "turnpass", h, direction, k, False).start()

    def last_arrivals(c):
        for k in (0, -1, 1, 2):
            for direction in range(2):
                for h in range(2):
                    ring(c, "turnpass", h, direction, k, True).wait_recv()

    def multiply(c, low, high):
        @pl.loop(low, high)
        def _(s):
            wide = gathered[c, s].astype(f32)
            normed = (wide * gain_ref[pl.ds(s, 1), :]).astype(bf16)
            squared = wide * wide
            folded = squared[:, :128]
            for part in range(1, width // 128):
                folded = folded + squared[:, part * 128 : (part + 1) * 128]
            squares[...] += folded
            total[...] += jnp.dot(normed, wkv[s], preferred_element_type=f32)

    def clear():
        total[...] = jnp.zeros_like(total)
        squares[...] = jnp.zeros_like(squares)

    def finish(c):
        scale = lax.rsqrt(jnp.sum(squares[...], axis=1, keepdims=True) / full_width + epsilon)
        span = pl.ds(c * piece, piece)
        key = (total[:, :width] * scale).astype(bf16)
        keys[:, span, :] = key.reshape(requests, piece, width)
        value = (total[:, width:] * scale).astype(bf16)
        values[:, span, :] = value.reshape(requests, piece, width)

    quarter_tp = n_tp // 4
    begin(0)
    for c in range(PIECES):
        middle(c)
        if c > 0:
            last_arrivals(c - 1)
            clear()
            multiply(c - 1, 0, quarter_tp)
        if c + 1 < PIECES:
            begin(c + 1)
        for i, k in enumerate((0, -1, 1, 2)):
            turn_arrivals(c, k)
            if c > 0 and i < 3:
                multiply(c - 1, (i + 1) * quarter_tp, (i + 2) * quarter_tp)
        if c > 0:
            finish(c - 1)
    last_arrivals(PIECES - 1)
    clear()
    multiply(PIECES - 1, 0, n_tp)
    finish(PIECES - 1)

    @pl.loop(0, requests)
    def _(j):
        scores = dot_t(spread, keys[j])
        most = jnp.maximum(own_most, jnp.max(scores, axis=1, keepdims=True))
        far = jnp.exp(scores - most)
        own = jnp.exp(own_scores - most)
        mass = jnp.sum(far, axis=1, keepdims=True) + jnp.sum(own, axis=1, keepdims=True)
        out = jnp.dot((far / mass).astype(bf16), values[j], preferred_element_type=f32)
        out += jnp.dot((own / mass).astype(bf16), own_value, preferred_element_type=f32)
        context = jnp.zeros((question_tokens, width), f32)
        for h in range(heads):
            block = out[h * question_tokens : (h + 1) * question_tokens]
            context = context + jnp.where(head_of == h, block, jnp.zeros_like(block))
        context_ref[j] = context.astype(bf16)

    @pl.loop(1, n_dp)
    def _(k):
        table_copy(k).wait_send()
        for c in range(PIECES):
            fetch_copy(c, k, d).wait_send()

    @pl.loop(1, n_tp)
    def _(k):
        asked_copy(k).wait_send()

    @pl.loop(0, PIECES)
    def _(c):
        for h in range(2):
            for direction in range(2):
                for kind in ("own", "pass"):
                    ring(c, kind, h, direction, 0, False).wait_send()
                for k in range(4):
                    for kind in ("turn", "turnpass"):
                        ring(c, kind, h, direction, k, False).wait_send()


def on_device(questions, memory, retrieved, location, norm_gain, w_query, w_key, w_value, w_out):
    n_dp, n_tp = lax.axis_size("dp"), lax.axis_size("tensor")
    question_count, question_tokens, width = questions.shape
    held, tokens, _ = memory.shape
    requests = retrieved.shape[1]
    heads_width = w_key.shape[1]
    piece = tokens // PIECES
    rows = requests * piece
    sem = pltpu.SemaphoreType.DMA
    vmem = pl.BlockSpec(memory_space=pltpu.VMEM)
    smem = pl.BlockSpec(memory_space=pltpu.SMEM)
    hbm = pl.BlockSpec(memory_space=pl.ANY)
    context = pl.pallas_call(
        functools.partial(attend_kernel, n_dp, n_tp),
        out_shape=jax.ShapeDtypeStruct((requests, question_tokens, heads_width), bf16),
        in_specs=[smem, smem, vmem, vmem, vmem, hbm, hbm, hbm],
        out_specs=vmem,
        scratch_shapes=[
            pltpu.VMEM((8, 128), jnp.int32),
            pltpu.VMEM((n_dp, 8, 128), jnp.int32),
            pltpu.SMEM((n_dp, 8, 128), jnp.int32),
            pltpu.SMEM((requests,), jnp.int32),
            pltpu.VMEM((PIECES, n_dp, SLOTS, piece, width), bf16),
            pltpu.VMEM((n_dp * SLOTS, piece, width), bf16),
            pltpu.VMEM((n_dp * SLOTS, piece, width), bf16),
            pltpu.VMEM((n_dp * SLOTS, piece, width), bf16),
            pltpu.VMEM((n_dp * SLOTS, piece, width), bf16),
            pltpu.VMEM((PIECES, n_tp, rows, width), bf16),
            pltpu.VMEM((n_tp, question_tokens, width), bf16),
            pltpu.VMEM((n_tp, width, heads_width), bf16),
            pltpu.VMEM((n_tp, width, 2 * heads_width), bf16),
            pltpu.VMEM((rows, 2 * heads_width), f32),
            pltpu.VMEM((rows, 128), f32),
            pltpu.VMEM((question_tokens, 3 * heads_width), f32),
            pltpu.VMEM((question_tokens, 128), f32),
            pltpu.VMEM((requests, tokens, heads_width), bf16),
            pltpu.VMEM((requests, tokens, heads_width), bf16),
            sem((3,)),
            sem,
            sem((n_dp,)),
            sem((n_dp,)),
            sem((n_tp,)),
            sem((n_tp,)),
            sem((PIECES, n_dp)),
            sem((PIECES, n_dp)),
            sem((PIECES, 40)),
            sem((PIECES, 40)),
        ],
        compiler_params=pltpu.CompilerParams(
            collective_id=0, has_side_effects=True, vmem_limit_bytes=56 * 1024 * 1024
        ),
        name="fetch_gather_attend",
    )(
        retrieved,
        location,
        questions.reshape(question_tokens, width),
        memory,
        norm_gain.reshape(n_tp, width),
        w_query.reshape(n_tp, width, heads_width),
        w_key.reshape(n_tp, width, heads_width),
        w_value.reshape(n_tp, width, heads_width),
    )
    context = context.reshape(requests * question_tokens, heads_width)
    head_term = jnp.dot(context, w_out, preferred_element_type=f32).astype(bf16)
    summed = lax.psum_scatter(head_term, "tensor", scatter_dimension=1, tiled=True).astype(f32)
    summed = summed.reshape(question_count, requests, question_tokens, width)
    return (questions.astype(f32)[:, None] + summed).astype(bf16)


def solution(mesh):
    placed = (
        P("dp", None, "tensor"),
        P("dp", None, "tensor"),
        P("dp", None),
        P(),
        P(),
        P(None, "tensor"),
        P(None, "tensor"),
        P(None, "tensor"),
        P("tensor", None),
    )
    return jax.shard_map(
        on_device,
        mesh=mesh,
        in_specs=placed,
        out_specs=P("dp", None, None, "tensor"),
        check_vma=False,
    )
```

time: 407 us -> 230 us (0.57)
  waiting for transfers between devices: 241 us -> 82.1 us
  Pallas kernels: 0 us -> 126 us
  blocking collectives: 80.5 us -> 0 us
  matrix products: 32.2 us -> 3.85 us
  other arithmetic: 19.5 us -> 1.68 us
  local copies, waits for them, and re-layouts: 18 us -> 2.17 us
    pallas_call x0 -> x1, Pallas kernels: none -> 126 us  [on_device(): pl.pallas_call(functools.partial(attend_kernel, n_dp, n_tp), out_shape=ja...]
    psum x1 -> x0, waiting for transfers between devices: 109 us -> none  [on_device(): lax.psum(head_term.astype(jnp.bfloat16), 'tensor').astype(jnp.float32)]
    all_gather x1 -> x0, waiting for transfers between devices: 46.9 us -> none  [on_device(): lax.all_gather(passage_rows, 'tensor', axis=1, tiled=True)]
    all_gather x2 -> x0, blocking collectives: 40.6 us -> none  [the longest x1 25.2 us: on_device(): lax.all_gather(question_rows, 'tensor', axis=1, tiled=True)]
    psum x1 -> x0, blocking collectives: 39.9 us -> none  [on_device(): lax.psum((jnp.sum(widened_question * widened_question, axis=1), jnp.sum(w...]
    dot_general x10 -> x1, matrix products: 32.2 us -> 3.85 us  [on_device(): head_term = jnp.dot(context, w_out, preferred_element_type=f32).astype(bf16)]
    select_n x3 -> x0, other arithmetic: 13.5 us -> none  [the longest x1 13.5 us: on_device(): jnp.where(held_here[:, None, None], picked, jnp.zeros((), jnp.bfloat16))]
    gather x2 -> x0, local copies, waits for them, and re-layouts: 11.2 us -> none  [the longest x1 9.2 us: on_device(): picked = memory[local_rows]]
  transfers between devices with their start and end apart: 3 -> 1, of which waited for: 3 -> 1; matrix products, arithmetic and copies ran while one was open for 2% -> 0% of each run, Pallas kernels for 0% -> 0%
where the time goes in v1:
time: 230 us; the launch traced here: 229 us
  Pallas kernels  126 us (55%)
  waiting for transfers between devices  82.1 us (36%)
  between operations  13.4 us (6%)
  matrix products  3.85 us (2%)
    pallas_call x1, Pallas kernels, on_device(): pl.pallas_call(functools.partial(attend_kernel, n_dp, n_tp), out_shape=ja...  126 us
    reduce_scatter x1, waiting for transfers between devices, on_device(): lax.psum_scatter(head_term, 'tensor', scatter_dimension=1, tiled=True)  82 us
  transfers between devices with their start and end apart: 1, of which 1 were waited for; matrix products, arithmetic and copies ran while one was open for 0% of the time, Pallas kernels for 0%

profile of v1, /device:TPU:32, one launch (start us, length us, event | category | flops | bytes accessed | tf_op | source)
XLA Modules:
  0.0 229.3 jit_solution(14446944231083166542)
XLA Ops:
  6.5 0.0 copy-start
  6.5 0.0 reduce-scatter.2.cloned.1.call-start
  6.5 1.5 reshape.42.gain_ref
  8.0 126.1 %fetch_gather_attend.1 = bf16[14,32,256]{2,1,0:T(8,128)(2,1)} custom-call(s32[1,14]{1,0:T(1,128)} %retrieved_ref.1, s32[256]{0:T(256)} %location_ref.1, bf16[32,256]{1,0:T(8,128)(2,1)} %bitcast.15, bf16[16,128,256]{2,1,0:T(8,128)(2,1)} %memory_ref.1, f32[16,256]{1,0:T(8,128)} %reshape.42.gain_ref, bf16[16,256,256]{2,1,0:T(8,128)(2,1)} %bitcast.10, ...), custom_call_target="tpu_custom_call" | custom-call | tf_op jit(solution)/shard_map/fetch_gather_attend/pallas_call | solution.py:399
  134.2 0.0 copy-done
  134.2 3.9 %convolution_convert_fusion = bf16[448,4096]{1,0:T(8,128)(2,1)} fusion(bf16[448,256]{1,0:T(8,128)(2,1)} %bitcast.13, bf16[256,4096]{1,0:T(8,128)(2,1)S(1)} %copy-done), kind=kOutput, calls=%fused_computation | convolution fusion | flops 941359104 | bytes 5996544 | tf_op jit(solution)/shard_map/dot_general | solution.py:450
  138.0 0.0 copy-start.1
  138.0 0.0 reduce-scatter.2.cloned.1.call-update
  138.0 0.7 copy-done.1
  138.7 82.0 %reduce-scatter.2.cloned.1.call-done = bf16[448,256]{1,0:T(8,128)(2,1)} async-done(((bf16[448,4096]{1,0:T(8,128)(2,1)}), bf16[448,256]{1,0:T(8,128)(2,1)}) %reduce-scatter.2.cloned.1.call-update) | async-done | bytes 229392 | tf_op jit(solution)/shard_map/reduce_scatter | solution.py:451
  220.8 1.7 fusion
  (1 shorter events, 0.0 us)
Async XLA Ops:
  6.5 127.6 %copy-start = (bf16[256,4096]{1,0:T(8,128)(2,1)S(1)}, bf16[256,4096]{1,0:T(8,128)(2,1)}, u32[]{:S(2)}) copy-start(bf16[256,4096]{1,0:T(8,128)(2,1)} %param.17) | copy-start | bytes 6291460
  6.5 214.3 %reduce-scatter.2.cloned.1.call-start = ((), (), s32[]{:S(2)}) async-start(), calls=%async_computation.1 | async-start | bytes 3899392 | tf_op jit(solution)/shard_map/reduce_scatter | solution.py:451
  138.0 0.7 copy-start.1
Sparse Core Ops, SparseCore 0:
  138.2 82.5 reduce-scatter.1

commit v2 on v1

--- a/solution.py
+++ b/solution.py
@@ -22,13 +22,17 @@
     n_tp,
     retrieved_ref,
     location_ref,
+    questions_hbm,
+    memory_hbm,
+    gain_hbm,
+    wq_hbm,
+    wk_hbm,
+    wv_hbm,
+    wo_hbm,
+    updated_ref,
     questions_ref,
     memory_ref,
     gain_ref,
-    wq_hbm,
-    wk_hbm,
-    wv_hbm,
-    context_ref,
     table,
     tables,
     tables_s,
@@ -42,6 +46,17 @@
     asked,
     wq,
     wkv,
+    wo,
+    contexts,
+    far_out,
+    far_in,
+    near_out,
+    near_in,
+    line_sum,
+    last_far_out,
+    last_far_in,
+    last_near_out,
+    last_near_in,
     total,
     squares,
     asked_total,
@@ -49,6 +64,7 @@
     keys,
     values,
     w_sem,
+    in_sem,
     tables_sem,
     table_send,
     table_recv,
@@ -58,6 +74,8 @@
     fetch_recv,
     ring_send,
     ring_recv,
+    sum_send,
+    sum_recv,
 ):
     inboxes = (inbox0, inbox1, inbox2, inbox3)
     held, tokens, width = memory_ref.shape
@@ -73,13 +91,25 @@
     t = lax.axis_index("tensor")
     x, y = lax.rem(t, SIDE), lax.div(t, SIDE)
 
+    def gain(s):
+        return gain_ref[:, pl.ds(pl.multiple_of(s * width, 128), width)]
+
     def at(dx, dy):
         return lax.rem(y + dy + SIDE, SIDE) * SIDE + lax.rem(x + dx + SIDE, SIDE)
+
+    in_copies = [
+        pltpu.make_async_copy(memory_hbm, memory_ref, in_sem.at[0]),
+        pltpu.make_async_copy(questions_hbm, questions_ref, in_sem.at[1]),
+        pltpu.make_async_copy(gain_hbm, gain_ref, in_sem.at[2]),
+    ]
+    for copy in in_copies:
+        copy.start()
 
     w_copies = [
         pltpu.make_async_copy(wq_hbm, wq, w_sem.at[0]),
         pltpu.make_async_copy(wk_hbm, wkv.at[:, :, pl.ds(0, width)], w_sem.at[1]),
         pltpu.make_async_copy(wv_hbm, wkv.at[:, :, pl.ds(width, width)], w_sem.at[2]),
+        pltpu.make_async_copy(wo_hbm, wo, w_sem.at[3]),
     ]
     for copy in w_copies:
         copy.start()
@@ -90,9 +120,9 @@
     def _(k):
         pl.semaphore_signal(barrier, inc=1, device_id={"dp": lax.rem(d + k, n_dp)}, device_id_type=MESH)
 
-    @pl.loop(1, n_tp)
-    def _(k):
-        pl.semaphore_signal(barrier, inc=1, device_id={"tensor": lax.rem(t + k, n_tp)}, device_id_type=MESH)
+    for k in range(1, SIDE):
+        pl.semaphore_signal(barrier, inc=1, device_id={"tensor": at(k, 0)}, device_id_type=MESH)
+        pl.semaphore_signal(barrier, inc=1, device_id={"tensor": at(0, k)}, device_id_type=MESH)
 
     stored = [location_ref[retrieved_ref[0, j]] for j in range(requests)]
     owners = [s // held for s in stored]
@@ -113,9 +143,10 @@
         place_s[j] = owners[j] * SLOTS + again
 
     tables[pl.ds(d, 1)] = table[...][None]
+    in_copies[1].wait()
     asked[pl.ds(t, 1)] = questions_ref[...][None]
 
-    pl.semaphore_wait(barrier, n_dp + n_tp - 2)
+    pl.semaphore_wait(barrier, n_dp - 1 + 2 * (SIDE - 1))
 
     def table_copy(k):
         return pltpu.make_async_remote_copy(
@@ -127,13 +158,19 @@
             device_id_type=MESH,
         )
 
-    def asked_copy(k):
+    def asked_copy(level, k, back):
+        if level == 0:
+            place = asked.at[at(-back, 0)]
+            target = at(k, 0)
+        else:
+            place = asked.at[pl.ds(lax.rem(y - back + SIDE, SIDE) * SIDE, SIDE)]
+            target = at(0, k)
         return pltpu.make_async_remote_copy(
-            src_ref=questions_ref,
-            dst_ref=asked.at[t],
-            send_sem=asked_send.at[k],
-            recv_sem=asked_recv.at[k],
-            device_id={"tensor": lax.rem(t + k, n_tp)},
+            src_ref=place,
+            dst_ref=place,
+            send_sem=asked_send.at[level * 3 + k - 1],
+            recv_sem=asked_recv.at[level * 3 + k - 1],
+            device_id={"tensor": target},
             device_id_type=MESH,
         )
 
@@ -147,23 +184,13 @@
             device_id_type=MESH,
         )
 
-    def asked_arrival(k):
-        return pltpu.make_async_remote_copy(
-            src_ref=questions_ref,
-            dst_ref=asked.at[lax.rem(t + n_tp - k, n_tp)],
-            send_sem=asked_send.at[k],
-            recv_sem=asked_recv.at[k],
-            device_id={"tensor": lax.rem(t + k, n_tp)},
-            device_id_type=MESH,
-        )
-
     @pl.loop(1, n_dp)
     def _(k):
         table_copy(k).start()
 
-    @pl.loop(1, n_tp)
-    def _(k):
-        asked_copy(k).start()
+    for k in range(1, SIDE):
+        asked_copy(0, k, 0).start()
+    in_copies[0].wait()
 
     @pl.loop(1, n_dp)
     def _(k):
@@ -196,39 +223,10 @@
         for s in range(SLOTS):
             inboxes[c][pl.ds(d * SLOTS + s, 1)] = memory_ref[tables_s[d, s, d], span, :][None]
 
-    for copy in w_copies:
-        copy.wait()
-
-    @pl.loop(1, n_tp)
-    def _(k):
-        asked_arrival(k).wait_recv()
-
-    asked_total[...] = jnp.zeros_like(asked_total)
-    asked_squares[...] = jnp.zeros_like(asked_squares)
-
-    @pl.loop(0, n_tp)
-    def _(s):
-        wide = asked[s].astype(f32)
-        normed = (wide * gain_ref[pl.ds(s, 1), :]).astype(bf16)
-        asked_squares[...] += jnp.sum(wide * wide, axis=1, keepdims=True)
-        asked_total[:, :width] += jnp.dot(normed, wq[s], preferred_element_type=f32)
-        asked_total[:, width:] += jnp.dot(normed, wkv[s], preferred_element_type=f32)
-
-    asked_scale = lax.rsqrt(asked_squares[:, :1] / full_width + epsilon)
-    projected = (asked_total[...] * asked_scale).astype(bf16)
-    own_query = projected[:, :width] * jnp.asarray(HEAD_DIM ** (-0.5), bf16)
-    own_key = projected[:, width : 2 * width]
-    own_value = projected[:, 2 * width :]
-    head_of = lax.broadcasted_iota(jnp.int32, (question_tokens, width), 1) // HEAD_DIM
-    spread = jnp.concatenate(
-        [jnp.where(head_of == h, own_query, jnp.zeros_like(own_query)) for h in range(heads)], axis=0
-    )
-
-    def dot_t(a, b):
-        return lax.dot_general(a, b, (((1,), (1,)), ((), ())), preferred_element_type=f32)
-
-    own_scores = dot_t(spread, own_key)
-    own_most = jnp.max(own_scores, axis=1, keepdims=True)
+    for k in range(1, SIDE):
+        asked_copy(0, k, k).wait_recv()
+    for k in range(1, SIDE):
+        asked_copy(1, k, 0).start()
 
     def ring(c, kind, h, direction, k, arrival):
         sign = 1 if direction == 0 else -1
@@ -273,23 +271,20 @@
         for h in range(2):
             for direction in range(2):
                 ring(c, "own", h, direction, 0, False).start()
-        for h in range(2):
-            for direction in range(2):
-                ring(c, "turn", h, direction, 0, False).start()
-
-    def middle(c):
-        for direction in range(2):
-            k = -1 if direction == 0 else 1
+
+    def along(c):
+        for direction in range(2):
             for h in range(2):
                 ring(c, "own", h, direction, 0, True).wait_recv()
                 ring(c, "pass", h, direction, 0, False).start()
-                for turned in range(2):
-                    ring(c, "turn", h, turned, k, False).start()
+
+    def turn(c, k):
         for h in range(2):
+            if k == 2:
+                for direction in range(2):
+                    ring(c, "pass", h, direction, 0, True).wait_recv()
             for direction in range(2):
-                ring(c, "pass", h, direction, 0, True).wait_recv()
-            for turned in range(2):
-                ring(c, "turn", h, turned, 2, False).start()
+                ring(c, "turn", h, direction, k, False).start()
 
     def turn_arrivals(c, k):
         for direction in range(2):
@@ -303,17 +298,20 @@
                 for h in range(2):
                     ring(c, "turnpass", h, direction, k, True).wait_recv()
 
-    def multiply(c, low, high):
+    def multiply(c, s):
+        wide = gathered[c, s].astype(f32)
+        normed = (wide * gain(s)).astype(bf16)
+        squared = wide * wide
+        folded = squared[:, :128]
+        for part in range(1, width // 128):
+            folded = folded + squared[:, part * 128 : (part + 1) * 128]
+        squares[...] += folded
+        total[...] += jnp.dot(normed, wkv[s], preferred_element_type=f32)
+
+    def multiply_range(c, low, high):
         @pl.loop(low, high)
         def _(s):
-            wide = gathered[c, s].astype(f32)
-            normed = (wide * gain_ref[pl.ds(s, 1), :]).astype(bf16)
-            squared = wide * wide
-            folded = squared[:, :128]
-            for part in range(1, width // 128):
-                folded = folded + squared[:, part * 128 : (part + 1) * 128]
-            squares[...] += folded
-            total[...] += jnp.dot(normed, wkv[s], preferred_element_type=f32)
+            multiply(c, s)
 
     def clear():
         total[...] = jnp.zeros_like(total)
@@ -327,41 +325,201 @@
         value = (total[:, width:] * scale).astype(bf16)
         values[:, span, :] = value.reshape(requests, piece, width)
 
+    def ask():
+        for copy in w_copies:
+            copy.wait()
+
+        in_copies[2].wait()
+        for k in range(1, SIDE):
+            asked_copy(1, k, k).wait_recv()
+
+        asked_total[...] = jnp.zeros_like(asked_total)
+        asked_squares[...] = jnp.zeros_like(asked_squares)
+
+        @pl.loop(0, n_tp)
+        def _(s):
+            wide = asked[s].astype(f32)
+            normed = (wide * gain(s)).astype(bf16)
+            asked_squares[...] += jnp.sum(wide * wide, axis=1, keepdims=True)
+            asked_total[:, :width] += jnp.dot(normed, wq[s], preferred_element_type=f32)
+            asked_total[:, width:] += jnp.dot(normed, wkv[s], preferred_element_type=f32)
+
     quarter_tp = n_tp // 4
+    last_piece = PIECES - 1
     begin(0)
     for c in range(PIECES):
-        middle(c)
-        if c > 0:
-            last_arrivals(c - 1)
+        along(c)
+        for k in (0, -1, 1):
+            turn(c, k)
+        if c == 0:
+            ask()
+        if c < last_piece:
+            begin(c + 1)
+        turn(c, 2)
+        if c > 1:
+            last_arrivals(c - 2)
             clear()
-            multiply(c - 1, 0, quarter_tp)
-        if c + 1 < PIECES:
-            begin(c + 1)
         for i, k in enumerate((0, -1, 1, 2)):
-            turn_arrivals(c, k)
-            if c > 0 and i < 3:
-                multiply(c - 1, (i + 1) * quarter_tp, (i + 2) * quarter_tp)
-        if c > 0:
-            finish(c - 1)
-    last_arrivals(PIECES - 1)
+            if c > 0:
+                turn_arrivals(c - 1, k)
+            if c > 1:
+                multiply_range(c - 2, i * quarter_tp, (i + 1) * quarter_tp)
+        if c > 1:
+            finish(c - 2)
+    last_arrivals(last_piece - 1)
     clear()
-    multiply(PIECES - 1, 0, n_tp)
-    finish(PIECES - 1)
-
-    @pl.loop(0, requests)
-    def _(j):
+    for i, k in enumerate((0, -1, 1, 2)):
+        turn_arrivals(last_piece, k)
+        multiply_range(last_piece - 1, i * quarter_tp, (i + 1) * quarter_tp)
+    finish(last_piece - 1)
+    clear()
+
+    @pl.loop(0, 9)
+    def _(i):
+        multiply(last_piece, at(lax.rem(i, 3) - 1, lax.div(i, 3) - 1))
+
+    last_arrivals(last_piece)
+
+    @pl.loop(0, 7)
+    def _(i):
+        multiply(last_piece, at(lax.select(i < 4, 2, i - 5), lax.select(i < 4, i - 1, 2)))
+
+    finish(last_piece)
+
+    asked_scale = lax.rsqrt(asked_squares[:, :1] / full_width + epsilon)
+    projected = (asked_total[...] * asked_scale).astype(bf16)
+    own_query = projected[:, :width] * jnp.asarray(HEAD_DIM ** (-0.5), bf16)
+    own_key = projected[:, width : 2 * width]
+    own_value = projected[:, 2 * width :]
+    head_of = lax.broadcasted_iota(jnp.int32, (question_tokens, width), 1) // HEAD_DIM
+    spread = jnp.concatenate(
+        [jnp.where(head_of == h, own_query, jnp.zeros_like(own_query)) for h in range(heads)], axis=0
+    )
+
+    def dot_t(a, b):
+        return lax.dot_general(a, b, (((1,), (1,)), ((), ())), preferred_element_type=f32)
+
+    own_scores = dot_t(spread, own_key)
+    own_most = jnp.max(own_scores, axis=1, keepdims=True)
+
+    def attend(j):
         scores = dot_t(spread, keys[j])
         most = jnp.maximum(own_most, jnp.max(scores, axis=1, keepdims=True))
         far = jnp.exp(scores - most)
         own = jnp.exp(own_scores - most)
         mass = jnp.sum(far, axis=1, keepdims=True) + jnp.sum(own, axis=1, keepdims=True)
-        out = jnp.dot((far / mass).astype(bf16), values[j], preferred_element_type=f32)
-        out += jnp.dot((own / mass).astype(bf16), own_value, preferred_element_type=f32)
+        share = 1.0 / mass
+        out = jnp.dot((far * share).astype(bf16), values[j], preferred_element_type=f32)
+        out += jnp.dot((own * share).astype(bf16), own_value, preferred_element_type=f32)
         context = jnp.zeros((question_tokens, width), f32)
         for h in range(heads):
             block = out[h * question_tokens : (h + 1) * question_tokens]
             context = context + jnp.where(head_of == h, block, jnp.zeros_like(block))
-        context_ref[j] = context.astype(bf16)
+        contexts[j] = context.astype(bf16)
+
+    part = requests // 2
+    part_rows = part * question_tokens
+    part_half = part_rows // 2
+
+    def aim(h, k1, k2):
+        return at(k1, k2) if h == 0 else at(k2, k1)
+
+    def term(h, low, count, s):
+        rows_in = contexts[h * part : (h + 1) * part].reshape(part_rows, width)[low : low + count]
+        columns = wo[:, pl.ds(pl.multiple_of(s * width, 128), width)]
+        return jnp.dot(rows_in, columns, preferred_element_type=f32)
+
+    def hop(kind, h, direction, k):
+        sign = 1 if direction == 0 else -1
+        k = k % 4
+        if kind == "far":
+            src, dst, index = far_out.at[h, direction, k], far_in.at[h, direction, k], direction * 4 + k
+        elif kind == "near":
+            src, dst, index = near_out.at[h, direction, k], near_in.at[h, direction, k], 8 + direction * 4 + k
+        elif kind == "last_far":
+            src, dst, index = last_far_out.at[h, direction], last_far_in.at[h, direction], 16 + direction
+        else:
+            src, dst, index = last_near_out.at[h, direction], last_near_in.at[h, direction], 18 + direction
+        target = aim(h, sign, 0) if kind in ("far", "near") else aim(h, 0, sign)
+        return pltpu.make_async_remote_copy(
+            src_ref=src,
+            dst_ref=dst,
+            send_sem=sum_send.at[h * 20 + index],
+            recv_sem=sum_recv.at[h * 20 + index],
+            device_id={"tensor": target},
+            device_id_type=MESH,
+        )
+
+    order = (2, 1, -1, 0)
+
+    def send_far(h):
+        for k in order:
+            for direction in range(2):
+                far_out[h, direction, k % 4] = term(h, direction * part_half, part_half, aim(h, 2, k)).astype(bf16)
+                hop("far", h, direction, k).start()
+
+    def send_near(h, k):
+        for direction in range(2):
+            sign = 1 if direction == 0 else -1
+            low = direction * part_half
+            here = term(h, 0, part_rows, aim(h, sign, k))
+            hop("far", h, direction, k).wait_recv()
+            passed = here[low : low + part_half] + far_in[h, direction, k % 4].astype(f32)
+            other = part_half - low
+            near_out[h, direction, k % 4, low : low + part_half] = passed.astype(bf16)
+            near_out[h, direction, k % 4, other : other + part_half] = here[other : other + part_half].astype(bf16)
+            hop("near", h, direction, k).start()
+
+    def sum_line(h, k):
+        here = term(h, 0, part_rows, aim(h, 0, k))
+        for direction in range(2):
+            hop("near", h, direction, k).wait_recv()
+            here = here + near_in[h, direction, k % 4].astype(f32)
+        line_sum[h, k % 4] = here
+
+    def send_last_far(h):
+        for direction in range(2):
+            low = direction * part_half
+            last_far_out[h, direction] = line_sum[h, 2, low : low + part_half].astype(bf16)
+            hop("last_far", h, direction, 0).start()
+
+    def send_last_near(h):
+        for direction in range(2):
+            k = 1 if direction == 0 else 3
+            low = direction * part_half
+            other = part_half - low
+            hop("last_far", h, direction, 0).wait_recv()
+            passed = line_sum[h, k, low : low + part_half] + last_far_in[h, direction].astype(f32)
+            last_near_out[h, direction, low : low + part_half] = passed.astype(bf16)
+            last_near_out[h, direction, other : other + part_half] = line_sum[h, k, other : other + part_half].astype(bf16)
+            hop("last_near", h, direction, 0).start()
+
+    def settle(h):
+        summed = line_sum[h, 0]
+        for direction in range(2):
+            hop("last_near", h, direction, 0).wait_recv()
+            summed = summed + last_near_in[h, direction].astype(f32)
+        summed = summed.reshape(part, question_tokens, width)
+        updated_ref[h * part : (h + 1) * part] = (questions_ref[...].astype(f32)[None] + summed).astype(bf16)
+
+    for h in range(2):
+
+        for j in range(h * part, (h + 1) * part):
+            attend(j)
+
+        send_far(h)
+    for k in order:
+        for h in range(2):
+            send_near(h, k)
+    for k in order:
+        for h in range(2):
+            sum_line(h, k)
+            if k == 2:
+                send_last_far(h)
+            if k == -1:
+                send_last_near(h)
+    for h in range(2):
+        settle(h)
 
     @pl.loop(1, n_dp)
     def _(k):
@@ -369,9 +527,9 @@
         for c in range(PIECES):
             fetch_copy(c, k, d).wait_send()
 
-    @pl.loop(1, n_tp)
-    def _(k):
-        asked_copy(k).wait_send()
+    for level in range(2):
+        for k in range(1, SIDE):
+            asked_copy(level, k, 0).wait_send()
 
     @pl.loop(0, PIECES)
     def _(c):
@@ -383,6 +541,14 @@
                     for kind in ("turn", "turnpass"):
                         ring(c, kind, h, direction, k, False).wait_send()
 
+    for h in range(2):
+        for direction in range(2):
+            for k in range(4):
+                for kind in ("far", "near"):
+                    hop(kind, h, direction, k).wait_send()
+            for kind in ("last_far", "last_near"):
+                hop(kind, h, direction, 0).wait_send()
+
 
 def on_device(questions, memory, retrieved, location, norm_gain, w_query, w_key, w_value, w_out):
     n_dp, n_tp = lax.axis_size("dp"), lax.axis_size("tensor")
@@ -392,16 +558,21 @@
     heads_width = w_key.shape[1]
     piece = tokens // PIECES
     rows = requests * piece
+    part_rows = (requests // 2) * question_tokens
+    part_half = part_rows // 2
     sem = pltpu.SemaphoreType.DMA
     vmem = pl.BlockSpec(memory_space=pltpu.VMEM)
     smem = pl.BlockSpec(memory_space=pltpu.SMEM)
     hbm = pl.BlockSpec(memory_space=pl.ANY)
-    context = pl.pallas_call(
+    updated = pl.pallas_call(
         functools.partial(attend_kernel, n_dp, n_tp),
-        out_shape=jax.ShapeDtypeStruct((requests, question_tokens, heads_width), bf16),
-        in_specs=[smem, smem, vmem, vmem, vmem, hbm, hbm, hbm],
+        out_shape=jax.ShapeDtypeStruct((requests, question_tokens, width), bf16),
+        in_specs=[smem, smem] + [hbm] * 7,
         out_specs=vmem,
         scratch_shapes=[
+            pltpu.VMEM((question_tokens, width), bf16),
+            pltpu.VMEM((held, tokens, width), bf16),
+            pltpu.VMEM((1, n_tp * width), f32),
             pltpu.VMEM((8, 128), jnp.int32),
             pltpu.VMEM((n_dp, 8, 128), jnp.int32),
             pltpu.SMEM((n_dp, 8, 128), jnp.int32),
@@ -415,42 +586,53 @@
             pltpu.VMEM((n_tp, question_tokens, width), bf16),
             pltpu.VMEM((n_tp, width, heads_width), bf16),
             pltpu.VMEM((n_tp, width, 2 * heads_width), bf16),
+            pltpu.VMEM((heads_width, n_tp * width), bf16),
+            pltpu.VMEM((requests, question_tokens, heads_width), bf16),
+            pltpu.VMEM((2, 2, SIDE, part_half, width), bf16),
+            pltpu.VMEM((2, 2, SIDE, part_half, width), bf16),
+            pltpu.VMEM((2, 2, SIDE, part_rows, width), bf16),
+            pltpu.VMEM((2, 2, SIDE, part_rows, width), bf16),
+            pltpu.VMEM((2, SIDE, part_rows, width), f32),
+            pltpu.VMEM((2, 2, part_half, width), bf16),
+            pltpu.VMEM((2, 2, part_half, width), bf16),
+            pltpu.VMEM((2, 2, part_rows, width), bf16),
+            pltpu.VMEM((2, 2, part_rows, width), bf16),
             pltpu.VMEM((rows, 2 * heads_width), f32),
             pltpu.VMEM((rows, 128), f32),
             pltpu.VMEM((question_tokens, 3 * heads_width), f32),
             pltpu.VMEM((question_tokens, 128), f32),
             pltpu.VMEM((requests, tokens, heads_width), bf16),
             pltpu.VMEM((requests, tokens, heads_width), bf16),
+            sem((4,)),
             sem((3,)),
             sem,
             sem((n_dp,)),
             sem((n_dp,)),
-            sem((n_tp,)),
-            sem((n_tp,)),
+            sem((6,)),
+            sem((6,)),
             sem((PIECES, n_dp)),
             sem((PIECES, n_dp)),
             sem((PIECES, 40)),
             sem((PIECES, 40)),
+            sem((40,)),
+            sem((40,)),
         ],
         compiler_params=pltpu.CompilerParams(
             collective_id=0, has_side_effects=True, vmem_limit_bytes=56 * 1024 * 1024
         ),
-        name="fetch_gather_attend",
+        name="attention_sublayer",
     )(
         retrieved,
         location,
         questions.reshape(question_tokens, width),
         memory,
-        norm_gain.reshape(n_tp, width),
+        norm_gain.reshape(1, n_tp * width),
         w_query.reshape(n_tp, width, heads_width),
         w_key.reshape(n_tp, width, heads_width),
         w_value.reshape(n_tp, width, heads_width),
+        w_out,
     )
-    context = context.reshape(requests * question_tokens, heads_width)
-    head_term = jnp.dot(context, w_out, preferred_element_type=f32).astype(bf16)
-    summed = lax.psum_scatter(head_term, "tensor", scatter_dimension=1, tiled=True).astype(f32)
-    summed = summed.reshape(question_count, requests, question_tokens, width)
-    return (questions.astype(f32)[:, None] + summed).astype(bf16)
+    return updated[None]
 
 
 def solution(mesh):

time: 230 us -> 150 us (0.65)
  waiting for transfers between devices: 82.1 us -> 0 us
  Pallas kernels: 126 us -> 147 us
  between operations: 13.4 us -> 0.01 us
  matrix products: 3.85 us -> 0 us
    reduce_scatter x1 -> x0, waiting for transfers between devices: 82 us -> none  [on_device(): lax.psum_scatter(head_term, 'tensor', scatter_dimension=1, tiled=True)]
    pallas_call x1, Pallas kernels: 126 us -> 147 us  [on_device(): pl.pallas_call(functools.partial(attend_kernel, n_dp, n_tp), out_shape=ja...]
    dot_general x1 -> x0, matrix products: 3.85 us -> none  [on_device(): head_term = jnp.dot(context, w_out, preferred_element_type=f32).astype(bf16)]
  transfers between devices with their start and end apart: 1 -> 0, of which waited for: 1 -> 0; matrix products, arithmetic and copies ran while one was open for 0% -> 0% of each run, Pallas kernels for 0% -> 0%
where the time goes in v2:
time: 150 us; the launch traced here: 149 us
  Pallas kernels  147 us (98%)
  local copies, waits for them, and re-layouts  1.64 us (1%)
    pallas_call x1, Pallas kernels, on_device(): pl.pallas_call(functools.partial(attend_kernel, n_dp, n_tp), out_shape=ja...  147 us

profile of v2, /device:TPU:32, one launch (start us, length us, event | category | flops | bytes accessed | tf_op | source)
XLA Modules:
  0.0 149.1 jit_solution(6862254250423627489)
XLA Ops:
  0.0 147.5 %attention_sublayer.1 = bf16[14,32,256]{2,1,0:T(8,128)(2,1)} custom-call(s32[1,14]{1,0:T(1,128)} %retrieved_ref.1, s32[256]{0:T(256)} %location_ref.1, bf16[32,256]{1,0:T(8,128)(2,1)} %bitcast.10, bf16[16,128,256]{2,1,0:T(8,128)(2,1)} %memory_hbm.1, f32[1,4096]{1,0:T(1,128)} %bitcast.11, bf16[16,256,256]{2,1,0:T(8,128)(2,1)} %bitcast.6, ...), custom_call_target="tpu_custom_call" | custom-call | tf_op jit(solution)/shard_map/attention_sublayer/pallas_call | solution.py:567
  147.5 1.6 %copy.11 = bf16[1,14,32,256]{3,2,1,0:T(8,128)(2,1)} copy(bf16[1,14,32,256]{3,2,1,0:T(8,128)(2,1)} %bitcast.9) | data formatting | bytes 458752

commit v3 on v2

--- a/solution.py
+++ b/solution.py
@@ -38,7 +38,9 @@
     tables_s,
     place_s,
     outbox,
-    inbox0,
+    held_kv,
+    outbox_kv,
+    inbox_kv,
     inbox1,
     inbox2,
     inbox3,
@@ -72,20 +74,23 @@
     asked_recv,
     fetch_send,
     fetch_recv,
+    kv_send,
+    kv_recv,
     ring_send,
     ring_recv,
     sum_send,
     sum_recv,
 ):
-    inboxes = (inbox0, inbox1, inbox2, inbox3)
+    inboxes = (None, inbox1, inbox2, inbox3)
     held, tokens, width = memory_ref.shape
     question_tokens = questions_ref.shape[0]
     requests = retrieved_ref.shape[1]
     piece = tokens // PIECES
-    rows = requests * piece
-    half = rows // 2
-    quarter = rows // 4
     full_width = n_tp * width
+
+    def rows_of(c):
+        return (held if c == 0 else requests) * piece
+
     heads = width // HEAD_DIM
     d = lax.axis_index("dp")
     t = lax.axis_index("tensor")
@@ -184,25 +189,9 @@
             device_id_type=MESH,
         )
 
-    @pl.loop(1, n_dp)
-    def _(k):
-        table_copy(k).start()
-
-    for k in range(1, SIDE):
-        asked_copy(0, k, 0).start()
-    in_copies[0].wait()
-
-    @pl.loop(1, n_dp)
-    def _(k):
-        table_arrival(k).wait_recv()
-
-    to_scalar = pltpu.make_async_copy(tables, tables_s, tables_sem)
-    to_scalar.start()
-    to_scalar.wait()
-
     def fetch_copy(c, k, sender):
         return pltpu.make_async_remote_copy(
-            src_ref=outbox.at[c, k],
+            src_ref=outbox.at[c - 1, k],
             dst_ref=inboxes[c].at[pl.ds(sender * SLOTS, SLOTS)],
             send_sem=fetch_send.at[c, k],
             recv_sem=fetch_recv.at[c, k],
@@ -210,23 +199,58 @@
             device_id_type=MESH,
         )
 
-    for c in range(PIECES):
+    def kv_copy(k, sender):
+        return pltpu.make_async_remote_copy(
+            src_ref=outbox_kv.at[k],
+            dst_ref=inbox_kv.at[pl.ds(sender * SLOTS, SLOTS)],
+            send_sem=kv_send.at[k],
+            recv_sem=kv_recv.at[k],
+            device_id={"dp": lax.rem(d + k, n_dp)},
+            device_id_type=MESH,
+        )
+
+    def read_tables():
+        @pl.loop(1, n_dp)
+        def _(k):
+            table_arrival(k).wait_recv()
+
+        to_scalar = pltpu.make_async_copy(tables, tables_s, tables_sem)
+        to_scalar.start()
+        to_scalar.wait()
+
+    def send_pieces(c):
         span = pl.ds(c * piece, piece)
 
         @pl.loop(1, n_dp)
         def _(k):
             asker = lax.rem(d + k, n_dp)
             for s in range(SLOTS):
-                outbox[c, k, s] = memory_ref[tables_s[asker, s, d], span, :]
+                outbox[c - 1, k, s] = memory_ref[tables_s[asker, s, d], span, :]
             fetch_copy(c, k, d).start()
 
         for s in range(SLOTS):
             inboxes[c][pl.ds(d * SLOTS + s, 1)] = memory_ref[tables_s[d, s, d], span, :][None]
 
-    for k in range(1, SIDE):
-        asked_copy(0, k, k).wait_recv()
-    for k in range(1, SIDE):
-        asked_copy(1, k, 0).start()
+    def send_kv():
+        @pl.loop(1, n_dp)
+        def _(k):
+            asker = lax.rem(d + k, n_dp)
+            for s in range(SLOTS):
+                outbox_kv[k, s] = held_kv[tables_s[asker, s, d]]
+            kv_copy(k, d).start()
+
+        for s in range(SLOTS):
+            inbox_kv[pl.ds(d * SLOTS + s, 1)] = held_kv[tables_s[d, s, d]][None]
+
+    def take_kv():
+        @pl.loop(1, n_dp)
+        def _(k):
+            kv_copy(k, lax.rem(d + n_dp - k, n_dp)).wait_recv()
+
+        for j in range(requests):
+            both = inbox_kv[place_s[j]]
+            keys[j, :piece] = both[:, :width]
+            values[j, :piece] = both[:, width:]
 
     def ring(c, kind, h, direction, k, arrival):
         sign = 1 if direction == 0 else -1
@@ -247,6 +271,8 @@
             shift = (k, 0) if h == 0 else (0, k)
             origin = at(*(b + s for b, s in zip(back, shift)))
             index = {"turn": 4, "turnpass": 12}[kind] + direction * 4 + k % 4
+        half = rows_of(c) // 2
+        quarter = half // 2
         if kind in ("pass", "turnpass"):
             span = pl.ds(h * half + direction * quarter, quarter)
         else:
@@ -262,12 +288,16 @@
         )
 
     def begin(c):
-        @pl.loop(1, n_dp)
-        def _(k):
-            fetch_copy(c, k, lax.rem(d + n_dp - k, n_dp)).wait_recv()
-
-        for j in range(requests):
-            gathered[c, pl.ds(t, 1), j * piece : (j + 1) * piece] = inboxes[c][place_s[j]][None]
+        if c == 0:
+            gathered[0, pl.ds(t, 1)] = memory_ref[:, :piece, :].reshape(1, held * piece, width)
+        else:
+
+            @pl.loop(1, n_dp)
+            def _(k):
+                fetch_copy(c, k, lax.rem(d + n_dp - k, n_dp)).wait_recv()
+
+            for j in range(requests):
+                gathered[c, pl.ds(t, 1), j * piece : (j + 1) * piece] = inboxes[c][place_s[j]][None]
         for h in range(2):
             for direction in range(2):
                 ring(c, "own", h, direction, 0, False).start()
@@ -299,14 +329,15 @@
                     ring(c, "turnpass", h, direction, k, True).wait_recv()
 
     def multiply(c, s):
-        wide = gathered[c, s].astype(f32)
+        rows = rows_of(c)
+        wide = gathered[c, s, :rows].astype(f32)
         normed = (wide * gain(s)).astype(bf16)
         squared = wide * wide
         folded = squared[:, :128]
         for part in range(1, width // 128):
             folded = folded + squared[:, part * 128 : (part + 1) * 128]
-        squares[...] += folded
-        total[...] += jnp.dot(normed, wkv[s], preferred_element_type=f32)
+        squares[:rows] += folded
+        total[:rows] += jnp.dot(normed, wkv[s], preferred_element_type=f32)
 
     def multiply_range(c, low, high):
         @pl.loop(low, high)
@@ -318,12 +349,16 @@
         squares[...] = jnp.zeros_like(squares)
 
     def finish(c):
-        scale = lax.rsqrt(jnp.sum(squares[...], axis=1, keepdims=True) / full_width + epsilon)
-        span = pl.ds(c * piece, piece)
-        key = (total[:, :width] * scale).astype(bf16)
-        keys[:, span, :] = key.reshape(requests, piece, width)
-        value = (total[:, width:] * scale).astype(bf16)
-        values[:, span, :] = value.reshape(requests, piece, width)
+        rows = rows_of(c)
+        scale = lax.rsqrt(jnp.sum(squares[:rows], axis=1, keepdims=True) / full_width + epsilon)
+        if c == 0:
+            held_kv[...] = (total[:rows] * scale).astype(bf16).reshape(held, piece, 2 * width)
+        else:
+            span = pl.ds(c * piece, piece)
+            key = (total[:rows, :width] * scale).astype(bf16)
+            keys[:, span, :] = key.reshape(requests, piece, width)
+            value = (total[:rows, width:] * scale).astype(bf16)
+            values[:, span, :] = value.reshape(requests, piece, width)
 
     def ask():
         for copy in w_copies:
@@ -346,25 +381,55 @@
 
     quarter_tp = n_tp // 4
     last_piece = PIECES - 1
+    shifts = (0, -1, 1, 2)
+
+    @pl.loop(1, n_dp)
+    def _(k):
+        table_copy(k).start()
+
+    in_copies[0].wait()
     begin(0)
-    for c in range(PIECES):
+    for k in range(1, SIDE):
+        asked_copy(0, k, 0).start()
+    along(0)
+    for k in (0, -1, 1):
+        turn(0, k)
+    read_tables()
+    send_pieces(1)
+    turn(0, 2)
+    send_pieces(2)
+    for k in range(1, SIDE):
+        asked_copy(0, k, k).wait_recv()
+    for k in range(1, SIDE):
+        asked_copy(1, k, 0).start()
+    send_pieces(3)
+    turn_arrivals(0, 0)
+    ask()
+    for k in (-1, 1, 2):
+        turn_arrivals(0, k)
+    begin(1)
+    for c in range(1, PIECES):
         along(c)
         for k in (0, -1, 1):
             turn(c, k)
-        if c == 0:
-            ask()
         if c < last_piece:
             begin(c + 1)
         turn(c, 2)
-        if c > 1:
+        if c == 1:
+            last_arrivals(0)
+            clear()
+            multiply_range(0, 0, n_tp)
+            finish(0)
+            send_kv()
+        if c > 2:
             last_arrivals(c - 2)
             clear()
-        for i, k in enumerate((0, -1, 1, 2)):
-            if c > 0:
+        for i, k in enumerate(shifts):
+            if c > 1:
                 turn_arrivals(c - 1, k)
-            if c > 1:
+            if c > 2:
                 multiply_range(c - 2, i * quarter_tp, (i + 1) * quarter_tp)
-        if c > 1:
+        if c > 2:
             finish(c - 2)
     last_arrivals(last_piece - 1)
     clear()
@@ -401,6 +466,8 @@
 
     own_scores = dot_t(spread, own_key)
     own_most = jnp.max(own_scores, axis=1, keepdims=True)
+
+    take_kv()
 
     def attend(j):
         scores = dot_t(spread, keys[j])
@@ -524,15 +591,15 @@
     @pl.loop(1, n_dp)
     def _(k):
         table_copy(k).wait_send()
-        for c in range(PIECES):
+        for c in range(1, PIECES):
             fetch_copy(c, k, d).wait_send()
+        kv_copy(k, d).wait_send()
 
     for level in range(2):
         for k in range(1, SIDE):
             asked_copy(level, k, 0).wait_send()
 
-    @pl.loop(0, PIECES)
-    def _(c):
+    for c in range(PIECES):
         for h in range(2):
             for direction in range(2):
                 for kind in ("own", "pass"):
@@ -557,7 +624,7 @@
     requests = retrieved.shape[1]
     heads_width = w_key.shape[1]
     piece = tokens // PIECES
-    rows = requests * piece
+    rows = max(held, requests) * piece
     part_rows = (requests // 2) * question_tokens
     part_half = part_rows // 2
     sem = pltpu.SemaphoreType.DMA
@@ -577,8 +644,10 @@
             pltpu.VMEM((n_dp, 8, 128), jnp.int32),
             pltpu.SMEM((n_dp, 8, 128), jnp.int32),
             pltpu.SMEM((requests,), jnp.int32),
-            pltpu.VMEM((PIECES, n_dp, SLOTS, piece, width), bf16),
-            pltpu.VMEM((n_dp * SLOTS, piece, width), bf16),
+            pltpu.VMEM((PIECES - 1, n_dp, SLOTS, piece, width), bf16),
+            pltpu.VMEM((held, piece, 2 * heads_width), bf16),
+            pltpu.VMEM((n_dp, SLOTS, piece, 2 * heads_width), bf16),
+            pltpu.VMEM((n_dp * SLOTS, piece, 2 * heads_width), bf16),
             pltpu.VMEM((n_dp * SLOTS, piece, width), bf16),
             pltpu.VMEM((n_dp * SLOTS, piece, width), bf16),
             pltpu.VMEM((n_dp * SLOTS, piece, width), bf16),
@@ -612,6 +681,8 @@
             sem((6,)),
             sem((PIECES, n_dp)),
             sem((PIECES, n_dp)),
+            sem((n_dp,)),
+            sem((n_dp,)),
             sem((PIECES, 40)),
             sem((PIECES, 40)),
             sem((40,)),

time: 150 us -> 136 us (0.907)
  Pallas kernels: 147 us -> 134 us
    pallas_call x1, Pallas kernels: 147 us -> 134 us  [on_device(): pl.pallas_call(functools.partial(attend_kernel, n_dp, n_tp), out_shape=ja...]
where the time goes in v3:
time: 136 us
  Pallas kernels  134 us (99%)
  local copies, waits for them, and re-layouts  1.64 us (1%)
    pallas_call x1, Pallas kernels, on_device(): pl.pallas_call(functools.partial(attend_kernel, n_dp, n_tp), out_shape=ja...  134 us

profile of v3, /device:TPU:32, one launch (start us, length us, event | category | flops | bytes accessed | tf_op | source)
XLA Modules:
  0.0 135.5 jit_solution(12766093517797462808)
XLA Ops:
  0.0 133.9 %attention_sublayer.1 = bf16[14,32,256]{2,1,0:T(8,128)(2,1)} custom-call(s32[1,14]{1,0:T(1,128)} %retrieved_ref.1, s32[256]{0:T(256)} %location_ref.1, bf16[32,256]{1,0:T(8,128)(2,1)} %bitcast.10, bf16[16,128,256]{2,1,0:T(8,128)(2,1)} %memory_hbm.1, f32[1,4096]{1,0:T(1,128)} %bitcast.11, bf16[16,256,256]{2,1,0:T(8,128)(2,1)} %bitcast.6, ...), custom_call_target="tpu_custom_call" | custom-call | tf_op jit(solution)/shard_map/attention_sublayer/pallas_call | solution.py:634
  133.9 1.6 %copy.11 = bf16[1,14,32,256]{3,2,1,0:T(8,128)(2,1)} copy(bf16[1,14,32,256]{3,2,1,0:T(8,128)(2,1)} %bitcast.9) | data formatting | bytes 458752

commit v4 on v3

--- a/solution.py
+++ b/solution.py
@@ -360,6 +360,11 @@
             value = (total[:rows, width:] * scale).astype(bf16)
             values[:, span, :] = value.reshape(requests, piece, width)
 
+    head_of = lax.broadcasted_iota(jnp.int32, (question_tokens, width), 1) // HEAD_DIM
+
+    def dot_t(a, b):
+        return lax.dot_general(a, b, (((1,), (1,)), ((), ())), preferred_element_type=f32)
+
     def ask():
         for copy in w_copies:
             copy.wait()
@@ -378,6 +383,19 @@
             asked_squares[...] += jnp.sum(wide * wide, axis=1, keepdims=True)
             asked_total[:, :width] += jnp.dot(normed, wq[s], preferred_element_type=f32)
             asked_total[:, width:] += jnp.dot(normed, wkv[s], preferred_element_type=f32)
+
+        asked_scale = lax.rsqrt(asked_squares[:, :1] / full_width + epsilon)
+        projected = (asked_total[...] * asked_scale).astype(bf16)
+        own_query = projected[:, :width] * jnp.asarray(HEAD_DIM ** (-0.5), bf16)
+        own_key = projected[:, width : 2 * width]
+        own_value = projected[:, 2 * width :]
+        spread = jnp.concatenate(
+            [jnp.where(head_of == h, own_query, jnp.zeros_like(own_query)) for h in range(heads)], axis=0
+        )
+
+        own_scores = dot_t(spread, own_key)
+        own_most = jnp.max(own_scores, axis=1, keepdims=True)
+        return spread, own_value, own_scores, own_most
 
     quarter_tp = n_tp // 4
     last_piece = PIECES - 1
@@ -404,33 +422,28 @@
         asked_copy(1, k, 0).start()
     send_pieces(3)
     turn_arrivals(0, 0)
-    ask()
-    for k in (-1, 1, 2):
-        turn_arrivals(0, k)
+    turn_arrivals(0, -1)
     begin(1)
-    for c in range(1, PIECES):
+    turn_arrivals(0, 1)
+    along(1)
+    turn_arrivals(0, 2)
+    for k in (0, -1, 1, 2):
+        turn(1, k)
+    spread, own_value, own_scores, own_most = ask()
+    begin(2)
+    for c in range(2, PIECES):
         along(c)
-        for k in (0, -1, 1):
-            turn(c, k)
         if c < last_piece:
             begin(c + 1)
-        turn(c, 2)
-        if c == 1:
-            last_arrivals(0)
-            clear()
-            multiply_range(0, 0, n_tp)
-            finish(0)
+        last_arrivals(c - 2)
+        clear()
+        for i, k in enumerate(shifts):
+            turn_arrivals(c - 1, k)
+            turn(c, k)
+            multiply_range(c - 2, i * quarter_tp, (i + 1) * quarter_tp)
+        finish(c - 2)
+        if c == 2:
             send_kv()
-        if c > 2:
-            last_arrivals(c - 2)
-            clear()
-        for i, k in enumerate(shifts):
-            if c > 1:
-                turn_arrivals(c - 1, k)
-            if c > 2:
-                multiply_range(c - 2, i * quarter_tp, (i + 1) * quarter_tp)
-        if c > 2:
-            finish(c - 2)
     last_arrivals(last_piece - 1)
     clear()
     for i, k in enumerate((0, -1, 1, 2)):
@@ -443,6 +456,7 @@
     def _(i):
         multiply(last_piece, at(lax.rem(i, 3) - 1, lax.div(i, 3) - 1))
 
+    take_kv()
     last_arrivals(last_piece)
 
     @pl.loop(0, 7)
@@ -450,24 +464,6 @@
         multiply(last_piece, at(lax.select(i < 4, 2, i - 5), lax.select(i < 4, i - 1, 2)))
 
     finish(last_piece)
-
-    asked_scale = lax.rsqrt(asked_squares[:, :1] / full_width + epsilon)
-    projected = (asked_total[...] * asked_scale).astype(bf16)
-    own_query = projected[:, :width] * jnp.asarray(HEAD_DIM ** (-0.5), bf16)
-    own_key = projected[:, width : 2 * width]
-    own_value = projected[:, 2 * width :]
-    head_of = lax.broadcasted_iota(jnp.int32, (question_tokens, width), 1) // HEAD_DIM
-    spread = jnp.concatenate(
-        [jnp.where(head_of == h, own_query, jnp.zeros_like(own_query)) for h in range(heads)], axis=0
-    )
-
-    def dot_t(a, b):
-        return lax.dot_general(a, b, (((1,), (1,)), ((), ())), preferred_element_type=f32)
-
-    own_scores = dot_t(spread, own_key)
-    own_most = jnp.max(own_scores, axis=1, keepdims=True)
-
-    take_kv()
 
     def attend(j):
         scores = dot_t(spread, keys[j])

time: 136 us -> 135 us (level)
  no operation moved by 1% of the time
where the time goes in v4:
time: 135 us
  Pallas kernels  133 us (99%)
  local copies, waits for them, and re-layouts  1.64 us (1%)
    pallas_call x1, Pallas kernels, on_device(): pl.pallas_call(functools.partial(attend_kernel, n_dp, n_tp), out_shape=ja...  133 us

profile of v4, /device:TPU:32, one launch (start us, length us, event | category | flops | bytes accessed | tf_op | source)
XLA Modules:
  0.0 134.7 jit_solution(14126711926738375256)
XLA Ops:
  0.0 133.0 %attention_sublayer.1 = bf16[14,32,256]{2,1,0:T(8,128)(2,1)} custom-call(s32[1,14]{1,0:T(1,128)} %retrieved_ref.1, s32[256]{0:T(256)} %location_ref.1, bf16[32,256]{1,0:T(8,128)(2,1)} %bitcast.10, bf16[16,128,256]{2,1,0:T(8,128)(2,1)} %memory_hbm.1, f32[1,4096]{1,0:T(1,128)} %bitcast.11, bf16[16,256,256]{2,1,0:T(8,128)(2,1)} %bitcast.6, ...), custom_call_target="tpu_custom_call" | custom-call | tf_op jit(solution)/shard_map/attention_sublayer/pallas_call | solution.py:630
  133.1 1.6 %copy.11 = bf16[1,14,32,256]{3,2,1,0:T(8,128)(2,1)} copy(bf16[1,14,32,256]{3,2,1,0:T(8,128)(2,1)} %bitcast.9) | data formatting | bytes 458752
